TPU v7x, 256 devices: a whole 4x4x8 slice. The times are simulated.
256 devices in a mesh: row: 16 (over z_hi, x), col: 16 (over y, z_lo, core).
Axes of the slice: x: 4, y: 4, z: 8 (z_hi: 4, z_lo: 2; z = z_hi * 2 + z_lo), core: 2. Of those that a mesh axis runs over, the one named last changes fastest.
Arguments:
- inputs: bfloat16 [2048, 16384], P('col', 'row'), may hold values from -0.13183594 to 0.13183594
- weight: bfloat16 [16384, 26624], P('row', 'col'), may hold values from -0.046875 to 0.046875
- grad_out: bfloat16 [2048, 26624], P('row', 'col'), may hold values from -6 to 6
Outputs:
- grad_inputs: bfloat16 [2048, 16384], P('col', 'row')
- grad_weight: bfloat16 [16384, 26624], P('row', 'col')
All inputs are finite; a program needn't handle non-finite values.
Results may differ from a plain program's by a relative error of at most 0.001.
Values may be sent and summed in bfloat16 or wider, within the bound.
A program may use at most 128 MiB of HBM per device.

v0:
```python
import jax
import jax.numpy as jnp
from jax import lax
from jax.sharding import PartitionSpec as P


def contract_tokens(left, right):
    return lax.dot_general(
        left, right, (((0,), (0,)), ((), ())), preferred_element_type=jnp.float32
    )


def contract_units(left, right):
    return lax.dot_general(
        left, right, (((1,), (1,)), ((), ())), preferred_element_type=jnp.float32
    )


def body(inputs, weight, grad_out):
    grad_rows = lax.all_gather(grad_out, "row", axis=0, tiled=True)
    grad_weight = contract_tokens(lax.all_gather(inputs, "col", axis=0, tiled=True), grad_rows)
    grad_inputs = lax.psum_scatter(
        contract_units(grad_rows, weight), "col", scatter_dimension=0, tiled=True
    ).astype(jnp.bfloat16)
    return (grad_inputs, grad_weight.astype(jnp.bfloat16))


def solution(mesh):
    return jax.shard_map(
        body,
        mesh=mesh,
        in_specs=(P("col", "row"), P("row", "col"), P("row", "col")),
        out_specs=(P("col", "row"), P("row", "col")),
        check_vma=False,
    )
```

profile of v0, /device:TPU:48, one launch (start us, length us, event | category | flops | bytes accessed | tf_op | source)
XLA Modules:
  0.0 262.9 jit_solution(14490339147225302818)
XLA Ops:
  7.2 0.0 copy-start
  7.2 0.0 all-gather.3.cloned.1.call-start
  7.2 0.7 all-gather.3.cloned.1.call-update
  7.9 0.0 all-gather.5.cloned.1.call-start
  8.0 0.7 all-gather.5.cloned.1.call-update
  8.7 0.0 reduce-scatter.2.cloned.1.call-start
  8.7 105.8 %all-gather.3.cloned.1.call-done = bf16[2048,1664]{1,0:T(8,128)(2,1)} async-done(((bf16[128,1664]{1,0:T(8,128)(2,1)}), bf16[2048,1664]{1,0:T(8,128)(2,1)}) %all-gather.3.cloned.1.call-update) | async-done | bytes 6815760 | tf_op jit(solution)/shard_map/all_gather | solution.py:20
  114.5 0.0 copy-done
  114.5 11.9 %fusion = f32[2048,1024]{1,0:T(8,128)} fusion(bf16[2048,1664]{1,0:T(8,128)(2,1)} %all-gather.3.cloned.1.call-done, bf16[1024,1664]{1,0:T(8,128)(2,1)S(1)} %copy-done), kind=kOutput, calls=%fused_computation.1 | convolution fusion | flops 6979321856 | bytes 18612224 | tf_op jit(solution)/shard_map/dot_general | solution.py:14
  126.4 0.0 reduce-scatter.2.cloned.1.call-update
  126.5 27.0 %all-gather.5.cloned.1.call-done = bf16[2048,1024]{1,0:T(8,128)(2,1)} async-done(((bf16[128,1024]{1,0:T(8,128)(2,1)}), bf16[2048,1024]{1,0:T(8,128)(2,1)}) %all-gather.5.cloned.1.call-update) | async-done | bytes 4194320 | tf_op jit(solution)/shard_map/all_gather | solution.py:21
  153.5 12.8 %convolution_convert_fusion = bf16[1024,1664]{1,0:T(8,128)(2,1)} fusion(bf16[2048,1024]{1,0:T(8,128)(2,1)} %all-gather.5.cloned.1.call-done, bf16[2048,1664]{1,0:T(8,128)(2,1)} %all-gather.3.cloned.1.call-done), kind=kOutput, calls=%fused_computation | convolution fusion | flops 6981025792 | bytes 14417920 | tf_op jit(solution)/shard_map/dot_general | solution.py:8
  166.3 88.3 %reduce-scatter.2.cloned.1.call-done = f32[128,1024]{1,0:T(8,128)} async-done(((f32[2048,1024]{1,0:T(8,128)}), f32[128,1024]{1,0:T(8,128)}) %reduce-scatter.2.cloned.1.call-update) | async-done | bytes 524304 | tf_op jit(solution)/shard_map/reduce_scatter | solution.py:22
  254.6 1.8 convert_element_type.6
Async XLA Ops:
  7.2 107.3 %copy-start = (bf16[1024,1664]{1,0:T(8,128)(2,1)S(1)}, bf16[1024,1664]{1,0:T(8,128)(2,1)}, u32[]{:S(2)}) copy-start(bf16[1024,1664]{1,0:T(8,128)(2,1)} %param.4) | copy-start | bytes 10223620
  7.2 107.3 %all-gather.3.cloned.1.call-start = ((), (), s32[]{:S(2)}) async-start(), calls=%async_computation.1 | async-start | bytes 7241728 | tf_op jit(solution)/shard_map/all_gather | solution.py:20
  7.9 145.6 %all-gather.5.cloned.1.call-start = ((), (), s32[]{:S(2)}) async-start(), calls=%async_computation.3 | async-start | bytes 4456448 | tf_op jit(solution)/shard_map/all_gather | solution.py:21
  8.7 245.9 %reduce-scatter.2.cloned.1.call-start = ((), (), s32[]{:S(2)}) async-start(), calls=%async_computation.2 | async-start | bytes 8912896 | tf_op jit(solution)/shard_map/reduce_scatter | solution.py:22
Sparse Core Ops, SparseCore 0:
  10.4 104.0 all-gather.2
  116.4 37.1 all-gather.4
  156.1 98.4 reduce-scatter.1
where the time goes:
time: 267 us; the launch traced here: 263 us
  waiting for transfers between devices  223 us (84%)
  matrix products  24.7 us (9%)
  between operations  13.8 us (5%)
    all_gather x1, waiting for transfers between devices, body(): grad_rows = lax.all_gather(grad_out, 'row', axis=0, tiled=True)  106 us
    reduce_scatter x1, waiting for transfers between devices, body(): lax.psum_scatter(contract_units(grad_rows, weight), 'col', scatter_dimens...  88.3 us
    all_gather x1, waiting for transfers between devices, body(): lax.all_gather(inputs, 'col', axis=0, tiled=True)  27 us
    dot_general x1, matrix products, contract_tokens(): lax.dot_general(left, right, (((0,), (0,)), ((), ())), preferred_element_...  12.8 us
    dot_general x1, matrix products, contract_units(): lax.dot_general(left, right, (((1,), (1,)), ((), ())), preferred_element_...  11.9 us
  transfers between devices with their start and end apart: 3, of which 3 were waited for; matrix products, arithmetic and copies ran while one was open for 9% of the time, Pallas kernels for 0%

commit v1 on v0

v1 whole, which is shorter than its diff:
```python
import functools

import jax
import jax.numpy as jnp
from jax import lax
from jax.experimental import pallas as pl
from jax.experimental.pallas import tpu as pltpu
from jax.sharding import PartitionSpec as P

MESH = pl.DeviceIdType.MESH

SLOTS = [
    (0, 0), (0, 1), (0, 3), (0, 2), (1, 0), (3, 0), (1, 1), (1, 3),
    (3, 1), (3, 3), (2, 0), (1, 2), (2, 1), (2, 3), (3, 2), (2, 2),
]
SLOT = {ij: s for s, ij in enumerate(SLOTS)}
EVEN = [s for s, (_, j) in enumerate(SLOTS) if j % 2 == 0]
ODD = [s for s, (_, j) in enumerate(SLOTS) if j % 2 == 1]
RANK = [EVEN.index(s) if s in EVEN else ODD.index(s) for s in range(16)]
LAG = 2


def table(index, values):
    out = jnp.int32(values[0])
    for at, value in enumerate(values[1:], 1):
        out = jnp.where(index == at, jnp.int32(value), out)
    return out


def kernel(
    in_ref, w_ref, go_ref, gin_ref, gw_ref,
    go, tin, w, acc, part, dbuf, ybuf, zbuf, stage, raw, gout,
    zs, zr, xs, xr, tys, tyr, tzs, tzr, tcs, tcr, ds, dr, ys, yr, rs, rr, ls, os,
):
    row, col = lax.axis_index("row"), lax.axis_index("col")
    zh, x = row // 4, lax.rem(row, 4)
    y, zl, core = col // 4, lax.rem(col // 2, 2), lax.rem(col, 2)
    tokens = raw.shape[0]
    half = tokens // 2
    width = tin.shape[1]

    def wrap(v):
        return lax.rem(v + 4, 4)

    def x_peer(d):
        return (zh * 4 + wrap(x + d), col)

    def z_peer(d):
        return (wrap(zh + d) * 4 + x, col)

    def kcol(yy, q, c):
        return (wrap(yy) * 2 + lax.rem(zl + q, 2)) * 2 + c

    def y_peer(d):
        return (row, kcol(y + d, 0, core))

    zl_peer = (row, kcol(y, 1, core))
    core_peer = (row, kcol(y, 0, 1 - core))

    def remote(src, dst, send, recv, to):
        return pltpu.make_async_remote_copy(
            src_ref=src, dst_ref=dst, send_sem=send, recv_sem=recv, device_id=to, device_id_type=MESH
        )

    def rows_of(slot, h):
        return pl.ds(slot * tokens + h * half, half)

    def z_copy(d, c):
        sign = 1 - 2 * d
        back = 3 if d == 0 else 1
        h = d if c != 1 else 1 - d
        src, dst = (SLOT[back, 0], SLOT[2, 0]) if c == 2 else (SLOT[0, 0], SLOT[back, 0])
        return remote(go.at[rows_of(src, h)], go.at[rows_of(dst, h)], zs.at[d, c], zr.at[d, c], z_peer(sign))

    def x_copy(i, d, c):
        sign = 1 - 2 * d
        back = 3 if d == 0 else 1
        h = d if c != 1 else 1 - d
        src, dst = (SLOT[i, back], SLOT[i, 2]) if c == 2 else (SLOT[i, 0], SLOT[i, back])
        return remote(go.at[rows_of(src, h)], go.at[rows_of(dst, h)], xs.at[i, d, c], xr.at[i, d, c], x_peer(sign))

    def t_copy(q, d, c):
        sign = 1 - 2 * d
        h = d if c != 1 else 1 - d
        k = kcol(y - sign, q, core) if c == 2 else kcol(y, q, core)
        part_of = tin.at[k, pl.ds(h * (width // 2), width // 2)]
        return remote(part_of, part_of, tys.at[q, d, c], tyr.at[q, d, c], y_peer(sign))

    def t_zl():
        block = tin.at[kcol(y, 0, core)]
        return remote(block, block, tzs, tzr, zl_peer)

    def t_core(q, e):
        if e < 3:
            block = tin.at[kcol(y + (0, 1, 3)[e], q, core)]
        else:
            block = tin.at[kcol(y + 2, q, core), pl.ds((e - 3) * (width // 2), width // 2)]
        return remote(block, block, tcs.at[q, e], tcr.at[q, e], core_peer)

    loads = [
        pltpu.make_async_copy(go_ref, go.at[pl.ds(0, tokens)], ls.at[0]),
        pltpu.make_async_copy(in_ref, raw, ls.at[1]),
        pltpu.make_async_copy(w_ref, w, ls.at[2]),
    ]
    for load in loads:
        load.start()

    barrier = pltpu.get_barrier_semaphore()
    for to in (x_peer(1), x_peer(3), z_peer(1), z_peer(3), y_peer(1), y_peer(3), zl_peer, core_peer):
        pl.semaphore_signal(barrier, inc=1, device_id=to, device_id_type=MESH)
    pl.semaphore_wait(barrier, 8)

    loads[0].wait()
    for c in range(2):
        for d in range(2):
            z_copy(d, c).start()
            x_copy(0, d, c).start()
    loads[1].wait()
    tin[kcol(y, 0, core)] = raw[...].T
    for c in range(2):
        for d in range(2):
            t_copy(0, d, c).start()
    t_core(0, 0).start()
    acc[...] = jnp.zeros_like(acc)
    loads[2].wait()

    def x_recv(i, c):
        for d in range(2):
            x_copy(i, d, c).wait_recv()

    def x_send(i, c):
        for d in range(2):
            x_copy(i, d, c).start()

    def t_far(q):
        for d in range(2):
            t_copy(q, d, 0).wait_recv()
        for d in range(2):
            t_copy(q, d, 2).start()
        for d in range(2):
            t_copy(q, d, 1).wait_recv()
            t_core(q, 2 - d).start()

    def t_far_core(q):
        for d in range(2):
            t_copy(q, d, 2).wait_recv()
            t_core(q, 3 + d).start()

    def before_1():
        x_recv(0, 0)
        x_send(0, 2)
        t_far(0)
        x_recv(0, 1)

    def before_3():
        for d in range(2):
            z_copy(d, 0).wait_recv()
        for d in range(2):
            z_copy(d, 2).start()
        x_copy(1, 0, 1).start()
        x_copy(1, 1, 0).start()
        x_copy(3, 0, 0).start()
        x_copy(3, 1, 1).start()
        t_zl().start()
        t_far_core(0)
        x_recv(0, 2)

    def before_4():
        for d in range(2):
            z_copy(d, 1).wait_recv()
        x_copy(1, 0, 0).start()
        x_copy(1, 1, 1).start()
        x_copy(3, 0, 1).start()
        x_copy(3, 1, 0).start()

    def before_6():
        x_recv(1, 0)
        x_recv(1, 1)
        x_send(1, 2)

    def before_8():
        for d in range(2):
            z_copy(d, 2).wait_recv()
        for c in range(2):
            x_send(2, c)
        x_recv(3, 0)
        x_recv(3, 1)
        x_send(3, 2)

    def before_10():
        t_zl().wait_recv()
        for c in range(2):
            for d in range(2):
                t_copy(1, d, c).start()
        t_core(1, 0).start()

    def before_11():
        x_recv(1, 2)

    def before_12():
        x_recv(2, 0)
        x_send(2, 2)
        t_far(1)
        x_recv(2, 1)

    def before_13():
        t_far_core(1)
        for q in range(2):
            for e in range(5):
                t_core(q, e).wait_recv()

    def before_14():
        x_recv(3, 2)

    def before_15():
        x_recv(2, 2)

    before = {
        1: before_1, 3: before_3, 4: before_4, 6: before_6, 8: before_8, 10: before_10,
        11: before_11, 12: before_12, 13: before_13, 14: before_14, 15: before_15,
    }

    def place(s):
        i, j = table(s, [i for i, _ in SLOTS]), table(s, [j for _, j in SLOTS])
        own = core == lax.rem(x + j, 2)
        return table(s, RANK), own, lax.rem(zh + i - y + 8, 4), wrap(x + j) // 2

    def d_copy(s, n):
        return remote(part.at[s], dbuf.at[n], ds.at[n], dr.at[n], core_peer)

    def y_copy(s, n, d, h):
        return remote(part.at[s, h], ybuf.at[n, d, h], ys.at[n, h], yr.at[n, d, h], y_peer(1 - 2 * d))

    def r_copy(s):
        return remote(part.at[s], zbuf, rs, rr, zl_peer)

    def share(s):
        block = go[pl.ds(pl.multiple_of(s * tokens, tokens), tokens), :]
        for h in range(2):
            part[s, h] = lax.dot_general(
                block, w[pl.ds(h * (width // 2), width // 2), :], (((1,), (1,)), ((), ())),
                preferred_element_type=jnp.float32,
            )

    def sum_cores(s):
        n, own, ahead, _ = place(s)

        @pl.when(own)
        def _():
            d_copy(s, n).wait_recv()
            part[s] += dbuf[n]

            @pl.when(ahead == 2)
            def _():
                y_copy(s, n, 0, 0).start()
                y_copy(s, n, 1, 1).start()

            @pl.when(ahead == 1)
            def _():
                y_copy(s, n, 0, 1).start()

            @pl.when(ahead == 3)
            def _():
                y_copy(s, n, 1, 0).start()

    def sum_far(s):
        n, own, ahead, _ = place(s)
        for d in range(2):

            @pl.when(jnp.logical_and(own, ahead == 1 + 2 * d))
            def _():
                y_copy(s, n, d, d).wait_recv()
                part[s, d] += ybuf[n, d, d]
                y_copy(s, n, d, d).start()

    def sum_near(s):
        n, own, ahead, z_to = place(s)

        @pl.when(jnp.logical_and(own, ahead == 0))
        def _():
            for d in range(2):
                for h in range(2):
                    y_copy(s, n, d, h).wait_recv()
            part[s] += ybuf[n, 0] + ybuf[n, 1]

            @pl.when(z_to != zl)
            def _():
                r_copy(s).start()

    tile = width // 4

    def out_copy(r):
        at = pl.ds(pl.multiple_of(r * tile, tile), tile)
        return pltpu.make_async_copy(stage.at[at], gw_ref.at[at], os.at[r])

    def weights(g):
        ks = []
        for e in range(4):
            i, j = (table(g, [SLOTS[4 * gg + e][axis] for gg in range(4)]) for axis in range(2))
            ks.append(wrap(zh + i) * 4 + wrap(x + j))

        def rows_tile(r, carry):
            at = pl.ds(pl.multiple_of(r * tile, tile), tile)
            left = jnp.concatenate([tin[k, at, :] for k in ks], axis=1)
            right = go[pl.ds(pl.multiple_of(g * 4 * tokens, 4 * tokens), 4 * tokens), :]
            acc[at, :] += lax.dot_general(
                left, right, (((1,), (0,)), ((), ())), preferred_element_type=jnp.float32
            )

            @pl.when(g == 3)
            def _():
                stage[at, :] = acc[at, :].astype(stage.dtype)
                out_copy(r).start()

            return carry

        lax.fori_loop(0, 4, rows_tile, 0)

    def step(s, carry):
        for at, event in before.items():
            pl.when(s == at)(event)

        @pl.when(s < 16)
        def _():
            share(s)
            n, own, _, _ = place(s)

            @pl.when(jnp.logical_not(own))
            def _():
                d_copy(s, n).start()

        @pl.when(jnp.logical_and(s >= LAG, s < 16 + LAG))
        def _():
            sum_far(s - LAG)

        @pl.when(s >= 2 * LAG)
        def _():
            sum_near(s - 2 * LAG)

        @pl.when(s < 16)
        def _():
            sum_cores(s)

        @pl.when(jnp.logical_and(s >= 13, s < 17))
        def _():
            weights(s - 13)

        return carry

    lax.fori_loop(0, 16 + 2 * LAG, step, 0)

    last_i, last_j = wrap(y - zh), wrap(zl * 2 + core - x)
    last = jnp.int32(0)
    for (i, j), s in SLOT.items():
        last = jnp.where(jnp.logical_and(last_i == i, last_j == j), jnp.int32(s), last)
    r_copy(last).wait_recv()
    for h in range(2):
        gout[:, h * (width // 2) : (h + 1) * (width // 2)] = (part[last, h] + zbuf[h]).astype(gout.dtype)
    give = pltpu.make_async_copy(gout, gin_ref, ls.at[3])
    give.start()

    for d in range(2):
        for c in range(3):
            z_copy(d, c).wait_send()
            for i in range(4):
                x_copy(i, d, c).wait_send()
            for q in range(2):
                t_copy(q, d, c).wait_send()
    t_zl().wait_send()
    for q in range(2):
        for e in range(5):
            t_core(q, e).wait_send()

    def drain(s, carry):
        n, own, ahead, _ = place(s)

        @pl.when(jnp.logical_not(own))
        def _():
            d_copy(s, n).wait_send()

        @pl.when(jnp.logical_and(own, ahead != 0))
        def _():
            for h in range(2):
                y_copy(s, n, 0, h).wait_send()

        return carry

    lax.fori_loop(0, 16, drain, 0)
    r_copy(last).wait_send()
    for r in range(4):
        out_copy(r).wait()
    give.wait()


def body(inputs, weight, grad_out):
    tokens, width = inputs.shape
    units = weight.shape[1]
    f32, bf16 = jnp.float32, jnp.bfloat16
    dma = pltpu.SemaphoreType.DMA
    return pl.pallas_call(
        kernel,
        out_shape=(
            jax.ShapeDtypeStruct((tokens, width), bf16),
            jax.ShapeDtypeStruct((width, units), bf16),
        ),
        in_specs=[pl.BlockSpec(memory_space=pl.ANY)] * 3,
        out_specs=[pl.BlockSpec(memory_space=pl.ANY)] * 2,
        scratch_shapes=[
            pltpu.VMEM((16 * tokens, units), bf16),
            pltpu.VMEM((16, width, tokens), bf16),
            pltpu.VMEM((width, units), bf16),
            pltpu.VMEM((width, units), f32),
            pltpu.VMEM((16, 2, tokens, width // 2), f32),
            pltpu.VMEM((8, 2, tokens, width // 2), f32),
            pltpu.VMEM((8, 2, 2, tokens, width // 2), f32),
            pltpu.VMEM((2, tokens, width // 2), f32),
            pltpu.VMEM((width, units), bf16),
            pltpu.VMEM((tokens, width), bf16),
            pltpu.VMEM((tokens, width), bf16),
            dma((2, 3)), dma((2, 3)),
            dma((4, 2, 3)), dma((4, 2, 3)),
            dma((2, 2, 3)), dma((2, 2, 3)),
            dma, dma,
            dma((2, 5)), dma((2, 5)),
            dma((8,)), dma((8,)),
            dma((8, 2)), dma((8, 2, 2)),
            dma, dma,
            dma((4,)), dma((4,)),
        ],
        compiler_params=pltpu.CompilerParams(
            collective_id=0, has_side_effects=True, vmem_limit_bytes=58 * 2**20
        ),
        cost_estimate=pl.CostEstimate(
            flops=4 * 16 * tokens * width * units, bytes_accessed=2 * 2 * width * units, transcendentals=0
        ),
        name="feed_forward_backward",
    )(inputs, weight, grad_out)


def solution(mesh):
    return jax.shard_map(
        body,
        mesh=mesh,
        in_specs=(P("col", "row"), P("row", "col"), P("row", "col")),
        out_specs=(P("col", "row"), P("row", "col")),
        check_vma=False,
    )
```

time: 267 us -> 119 us (0.45); the launches traced: 263 us -> 119 us
  waiting for transfers between devices: 223 us -> 0 us
  Pallas kernels: 0 us -> 112 us
  matrix products: 24.7 us -> 0 us
  between operations: 13.8 us -> 0.64 us
  local copies, waits for them, and re-layouts: 0.01 us -> 5.63 us
    all_gather x2 -> x0, waiting for transfers between devices: 133 us -> none  [the longest x1 106 us: body(): grad_rows = lax.all_gather(grad_out, 'row', axis=0, tiled=True)]
    pallas_call x0 -> x1, Pallas kernels: none -> 112 us  [body(): pl.pallas_call(kernel, out_shape=(jax.ShapeDtypeStruct((tokens, width), b...]
    reduce_scatter x1 -> x0, waiting for transfers between devices: 88.3 us -> none  [body(): lax.psum_scatter(contract_units(grad_rows, weight), 'col', scatter_dimens...]
    dot_general x2 -> x0, matrix products: 24.7 us -> none  [the longest x1 12.8 us: contract_tokens(): lax.dot_general(left, right, (((0,), (0,)), ((), ())), preferred_element_...]
    unnamed x2, local copies, waits for them, and re-layouts: 0.01 us -> 5.63 us
  transfers between devices with their start and end apart: 3 -> 0, of which waited for: 3 -> 0; matrix products, arithmetic and copies ran while one was open for 9% -> 0% of each run, Pallas kernels for 0% -> 0%
where the time goes in v1:
time: 119 us
  Pallas kernels  112 us (94%)
  local copies, waits for them, and re-layouts  5.63 us (5%)
    pallas_call x1, Pallas kernels, body(): pl.pallas_call(kernel, out_shape=(jax.ShapeDtypeStruct((tokens, width), b...  112 us
    unnamed x2, local copies, waits for them, and re-layouts  5.63 us

profile of v1, /device:TPU:48, one launch (start us, length us, event | category | flops | bytes accessed | tf_op | source)
XLA Modules:
  0.0 118.6 jit_solution(11386620954758340482)
XLA Ops:
  0.6 112.3 %feed_forward_backward.1 = (bf16[128,1024]{1,0:T(8,128)(2,1)}, bf16[1024,1664]{1,0:T(8,128)(2,1)}) custom-call(bf16[128,1024]{1,0:T(8,128)(2,1)} %in_ref.1, bf16[1024,1664]{1,0:T(8,128)(2,1)} %w_ref.1, bf16[128,1664]{1,0:T(8,128)(2,1)} %go_ref.1), custom_call_target="tpu_custom_call" | custom-call | flops 13958643712 | bytes 6815744 | tf_op jit(solution)/shard_map/feed_forward_backward/pallas_call | solution.py:400
  113.0 1.7 %copy.7 = bf16[128,1024]{1,0:T(8,128)(2,1)} copy(bf16[128,1024]{1,0:T(8,128)(2,1)} %get-tuple-element.4) | data formatting | bytes 524288
  114.6 4.0 %copy.8 = bf16[1024,1664]{1,0:T(8,128)(2,1)} copy(bf16[1024,1664]{1,0:T(8,128)(2,1)} %get-tuple-element.5) | data formatting | bytes 6815744

commit v2 on v0

v2 whole, which is shorter than its diff:
```python
import jax
import jax.numpy as jnp
from jax import lax
from jax.experimental import pallas as pl
from jax.experimental.pallas import tpu as pltpu
from jax.sharding import PartitionSpec as P

MESH = pl.DeviceIdType.MESH
PIECES = 4

SLOTS = [
    (0, 0), (0, 1), (0, 3), (0, 2), (1, 0), (3, 0), (1, 1), (1, 3),
    (3, 1), (3, 3), (2, 0), (1, 2), (2, 1), (2, 3), (3, 2), (2, 2),
]
SLOT = {ij: s for s, ij in enumerate(SLOTS)}
EVEN = [s for s, (_, j) in enumerate(SLOTS) if j % 2 == 0]
ODD = [s for s, (_, j) in enumerate(SLOTS) if j % 2 == 1]
RANK = [EVEN.index(s) if s in EVEN else ODD.index(s) for s in range(16)]

ORDER = [
    ("tf", 0, 0), ("tc", 0, 0), ("tf", 0, 1), ("fx", 0, 0), ("P", 0), ("fx", 0, 1), ("xa3",), ("xa1",), ("P", 1),
    ("tl",), ("C", 1), ("P", 2), ("xb3",), ("zf", 1), ("P", 4), ("xb1",), ("fx", 3, 0), ("zf", 0), ("tr",),
    ("tc", 0, 1), ("tg", 0, 1), ("C", 4), ("P", 5), ("P", 3), ("C", 5), ("P", 9), ("fx", 1, 1), ("tf", 1, 0),
    ("tf", 1, 1), ("g", 1), ("C", 3), ("P", 8), ("g", 0), ("P", 6), ("C", 9), ("xa2",), ("P", 7), ("tc", 1, 0),
    ("C", 6), ("C", 8), ("tg", 1, 1), ("C", 7), ("P", 10), ("C", 10), ("C", 0), ("tg", 0, 0), ("xb2",),
    ("tg", 1, 0), ("F", 3), ("F", 9), ("F", 4), ("P", 11), ("P", 12), ("C", 11), ("fx", 2, 0), ("F", 5), ("F", 10),
    ("tc", 1, 1), ("C", 12), ("fx", 2, 1), ("F", 8), ("P", 14), ("G", 0, 0), ("F", 1), ("G", 0, 1), ("P", 13),
    ("N", 5), ("N", 3), ("C", 2), ("N", 9), ("C", 14), ("F", 11), ("F", 12), ("P", 15), ("N", 4), ("G", 0, 2),
    ("C", 15), ("F", 2), ("G", 0, 3), ("G", 1, 0), ("F", 15), ("G", 1, 1), ("N", 8), ("N", 10), ("N", 12), ("F", 0),
    ("C", 13), ("F", 7), ("F", 13), ("N", 11), ("N", 1), ("F", 14), ("G", 1, 2), ("G", 1, 3), ("F", 6), ("G", 2, 0),
    ("N", 15), ("N", 7), ("N", 2), ("G", 2, 1), ("N", 6), ("G", 2, 2), ("N", 0), ("N", 14), ("G", 2, 3),
    ("G", 3, 0), ("G", 3, 1), ("N", 13), ("G", 3, 2), ("G", 3, 3),
]


def table(index, values):
    out = jnp.int32(values[0])
    for at, value in enumerate(values[1:], 1):
        if value != values[0]:
            out = jnp.where(index == at, jnp.int32(value), out)
    return out


def kernel(
    in_ref, w_ref, go_ref, gin_ref, gw_ref,
    go, tin, w, acc, part, dbuf, ybuf, zbuf, stage, raw, gout,
    zs, zr, xs, xr, tys, tyr, tzs, tzr, tcs, tcr, ds, dr, ys, yr, rs, rr, ls, os,
):
    row, col = lax.axis_index("row"), lax.axis_index("col")
    zh, x = row // 4, lax.rem(row, 4)
    y, zl, core = col // 4, lax.rem(col // 2, 2), lax.rem(col, 2)
    tokens = raw.shape[0]
    half = tokens // 2
    width = tin.shape[1]
    piece = width // PIECES

    def wrap(v):
        return lax.rem(v + 4, 4)

    def x_peer(d):
        return (zh * 4 + wrap(x + d), col)

    def z_peer(d):
        return (wrap(zh + d) * 4 + x, col)

    def kcol(yy, q, c):
        return (wrap(yy) * 2 + lax.rem(zl + q, 2)) * 2 + c

    def y_peer(d):
        return (row, kcol(y + d, 0, core))

    zl_peer = (row, kcol(y, 1, core))
    core_peer = (row, kcol(y, 0, 1 - core))

    def remote(src, dst, send, recv, to):
        return pltpu.make_async_remote_copy(
            src_ref=src, dst_ref=dst, send_sem=send, recv_sem=recv, device_id=to, device_id_type=MESH
        )

    def rows_of(slot, h):
        return pl.ds(slot * tokens + h * half, half)

    def z_copy(d, c):
        sign, back = 1 - 2 * d, 3 - 2 * d
        h = d if c in (0, 2) else 1 - d
        src, dst = {2: ((back, 0), (2, 0)), 3: ((0, 2), (back, 2))}.get(c, ((0, 0), (back, 0)))
        return remote(
            go.at[rows_of(SLOT[src], h)], go.at[rows_of(SLOT[dst], h)], zs.at[d, c], zr.at[d, c], z_peer(sign)
        )

    def x_copy(i, d, c):
        sign, back = 1 - 2 * d, 3 - 2 * d
        h = d if c != 1 else 1 - d
        src, dst = ((i, back), (i, 2)) if c == 2 else ((i, 0), (i, back))
        return remote(
            go.at[rows_of(SLOT[src], h)], go.at[rows_of(SLOT[dst], h)], xs.at[i, d, c], xr.at[i, d, c], x_peer(sign)
        )

    def t_copy(q, d, c):
        sign = 1 - 2 * d
        h = d if c != 1 else 1 - d
        k = kcol(y - sign, q, core) if c == 2 else kcol(y, q, core)
        block = tin.at[k, pl.ds(h * (width // 2), width // 2)]
        return remote(block, block, tys.at[q, d, c], tyr.at[q, d, c], y_peer(sign))

    def t_zl():
        block = tin.at[kcol(y, 0, core)]
        return remote(block, block, tzs, tzr, zl_peer)

    def t_core(q, e):
        if e < 3:
            block = tin.at[kcol(y + (0, 1, 3)[e], q, core)]
        else:
            block = tin.at[kcol(y + 2, q, core), pl.ds((e - 3) * (width // 2), width // 2)]
        return remote(block, block, tcs.at[q, e], tcr.at[q, e], core_peer)

    def place(s):
        if isinstance(s, int):
            (i, j), rank = SLOTS[s], RANK[s]
        else:
            i, j, rank = table(s, [i for i, _ in SLOTS]), table(s, [j for _, j in SLOTS]), table(s, RANK)
        own = core == lax.rem(x + j, 2)
        return rank, own, lax.rem(zh + i - y + 8, 4), wrap(x + j) // 2

    def d_copy(s, n):
        return remote(part.at[s], dbuf.at[n], ds.at[n], dr.at[n], core_peer)

    def y_copy(s, n, d, p):
        return remote(part.at[s, p], ybuf.at[n, d, p], ys.at[n, p], yr.at[n, d, p], y_peer(1 - 2 * d))

    def r_copy(s, p):
        return remote(part.at[s, p], zbuf.at[p], rs.at[p], rr.at[p], zl_peer)

    loads = [
        pltpu.make_async_copy(go_ref, go.at[pl.ds(0, tokens)], ls.at[0]),
        pltpu.make_async_copy(in_ref, raw, ls.at[1]),
        pltpu.make_async_copy(w_ref, w, ls.at[2]),
    ]
    for load in loads:
        load.start()

    barrier = pltpu.get_barrier_semaphore()
    for to in (x_peer(1), x_peer(3), z_peer(1), z_peer(3), y_peer(1), y_peer(3), zl_peer, core_peer):
        pl.semaphore_signal(barrier, inc=1, device_id=to, device_id_type=MESH)
    pl.semaphore_wait(barrier, 8)

    loads[0].wait()
    for c in range(2):
        for d in range(2):
            z_copy(d, c).start()
            x_copy(0, d, c).start()
    loads[1].wait()
    tin[kcol(y, 0, core)] = raw[...].T
    for c in range(2):
        for d in range(2):
            t_copy(0, d, c).start()
    t_core(0, 0).start()
    acc[...] = jnp.zeros_like(acc)
    loads[2].wait()

    arrivals = {"x": x_copy, "z": z_copy, "t": t_copy, "tl": t_zl, "tc": t_core}
    met = set()
    sent = [("z", d, c) for d in range(2) for c in range(2)]
    sent += [("x", 0, d, c) for d in range(2) for c in range(2)]
    sent += [("t", 0, d, c) for d in range(2) for c in range(2)] + [("tc", 0, 0)]

    def need(*names):
        for name in names:
            if name not in met:
                met.add(name)
                arrivals[name[0]](*name[1:]).wait_recv()

    def begin(*names):
        for name in names:
            sent.append(name)
            arrivals[name[0]](*name[1:]).start()

    def need_block(s):
        i, j = SLOTS[s]
        if j == 0:
            need(*{0: [], 1: [("z", 1, 0), ("z", 1, 1)], 3: [("z", 0, 0), ("z", 0, 1)], 2: [("z", 0, 2), ("z", 1, 2)]}[i])
        elif j != 2:
            need(("x", i, (j == 1) * 1, 0), ("x", i, (j == 1) * 1, 1))
        else:
            for d in range(2):
                passed = ("fx", i, d) in ORDER
                need(("x", i, d, 2) if passed else ("z", 1 - d, 3))

    def sum_cores(s):
        n, own, ahead, _ = place(s)

        @pl.when(own)
        def _():
            d_copy(s, n).wait_recv()

            def add(p, carry):
                part[s, p] += dbuf[n, p]
                return carry

            lax.fori_loop(0, PIECES, add, 0)

            @pl.when(ahead == 2)
            def _():
                for p in range(PIECES // 2):
                    y_copy(s, n, 0, p).start()
                    y_copy(s, n, 1, PIECES // 2 + p).start()

            @pl.when(jnp.logical_or(ahead == 1, ahead == 3))
            def _():
                d = ahead // 2
                for p in range(PIECES // 2):
                    y_copy(s, n, d, (1 - d) * (PIECES // 2) + p).start()

    def sum_far(s):
        n, own, ahead, _ = place(s)

        @pl.when(jnp.logical_and(own, jnp.logical_or(ahead == 1, ahead == 3)))
        def _():
            d = ahead // 2

            def add(e, carry):
                p = d * (PIECES // 2) + e
                y_copy(s, n, d, p).wait_recv()
                part[s, p] += ybuf[n, d, p]
                y_copy(s, n, d, p).start()
                return carry

            lax.fori_loop(0, PIECES // 2, add, 0)

    def sum_near(s):
        n, own, ahead, z_to = place(s)

        @pl.when(jnp.logical_and(own, ahead == 0))
        def _():
            def add(e, carry):
                p = e // 2 + lax.rem(e, 2) * (PIECES // 2)
                for d in range(2):
                    y_copy(s, n, d, p).wait_recv()
                part[s, p] += ybuf[n, 0, p] + ybuf[n, 1, p]

                @pl.when(z_to != zl)
                def _():
                    r_copy(s, p).start()

                return carry

            lax.fori_loop(0, PIECES, add, 0)

    def light(kind, *at):
        if kind == "fx":
            need(("x", *at, 0))
            begin(("x", *at, 2))
        elif kind == "zf":
            need(("z", *at, 0))
            begin(("z", *at, 2))
        elif kind in ("xa1", "xb1", "xa3", "xb3", "xa2", "xb2"):
            i = int(kind[2])
            later = kind[1] == "b"
            need({1: ("z", 1, later * 1), 3: ("z", 0, later * 1), 2: ("z", later * 1, 2)}[i])
            upper = later == (i != 1)
            begin(("x", i, 0, upper * 1), ("x", i, 1, 1 - upper))
        elif kind == "g":
            need(("x", 0, 1 - at[0], 2))
            begin(("z", at[0], 3))
        elif kind == "tl":
            begin(("tl",))
        elif kind == "tr":
            need(("tl",))
            begin(*[("t", 1, d, c) for c in range(2) for d in range(2)], ("tc", 1, 0))
        elif kind == "tf":
            need(("t", *at, 0))
            begin(("t", *at, 2))
        elif kind == "tc":
            need(("t", *at, 0), ("t", *at, 1))
            begin(("tc", at[0], 2 - at[1]))
        elif kind == "tg":
            need(("t", *at, 2))
            begin(("tc", at[0], 3 + at[1]))
        else:
            {"C": sum_cores, "F": sum_far, "N": sum_near}[kind](*at)

    def share(s):
        block = go[pl.ds(pl.multiple_of(s * tokens, tokens), tokens), :]
        for h in range(2):
            both = lax.dot_general(
                block, w[pl.ds(h * (width // 2), width // 2), :], (((1,), (1,)), ((), ())),
                preferred_element_type=jnp.float32,
            )
            for e in range(PIECES // 2):
                part[s, h * (PIECES // 2) + e] = both[:, e * piece : (e + 1) * piece]
        n, own, _, _ = place(s)

        @pl.when(jnp.logical_not(own))
        def _():
            d_copy(s, n).start()

    tile = width // 4

    def out_copy(r):
        at = pl.ds(pl.multiple_of(r * tile, tile), tile)
        return pltpu.make_async_copy(stage.at[at], gw_ref.at[at], os.at[r])

    def weights(g, r):
        ks = []
        for e in range(4):
            i, j = (table(g, [SLOTS[4 * gg + e][axis] for gg in range(4)]) for axis in range(2))
            ks.append(wrap(zh + i) * 4 + wrap(x + j))
        at = pl.ds(pl.multiple_of(r * tile, tile), tile)
        left = jnp.concatenate([tin[k, at, :] for k in ks], axis=1)
        right = go[pl.ds(pl.multiple_of(g * 4 * tokens, 4 * tokens), 4 * tokens), :]
        acc[at, :] += lax.dot_general(left, right, (((1,), (0,)), ((), ())), preferred_element_type=jnp.float32)

        @pl.when(g == 3)
        def _():
            stage[at, :] = acc[at, :].astype(stage.dtype)
            out_copy(r).start()

    heavy = [t for t in ORDER if t[0] in "PG"]
    before, waiting = [], []
    for t in ORDER:
        if t[0] in "PG":
            before.append(waiting)
            waiting = []
        else:
            waiting.append(t)

    def step(h, carry):
        for at, tasks in enumerate(before):

            @pl.when(h == at)
            def _():
                for t in tasks:
                    light(*t)
                if heavy[at][0] == "P":
                    need_block(heavy[at][1])
                else:
                    need(*[("t", q, d, c) for q in range(2) for d in range(2) for c in range(3)], ("tl",))
                    need(*[("tc", q, e) for q in range(2) for e in range(5)])
                    for s in range(4 * heavy[at][1], 4 * heavy[at][1] + 4):
                        need_block(s)

        is_share = table(h, [t[0] == "P" for t in heavy]) == 1

        @pl.when(is_share)
        def _():
            share(table(h, [t[1] if t[0] == "P" else 0 for t in heavy]))

        @pl.when(jnp.logical_not(is_share))
        def _():
            weights(
                table(h, [t[1] if t[0] == "G" else 0 for t in heavy]),
                table(h, [t[2] if t[0] == "G" else 0 for t in heavy]),
            )

        return carry

    lax.fori_loop(0, len(heavy), step, 0)
    for t in waiting:
        light(*t)

    last_i, last_j = wrap(y - zh), wrap(zl * 2 + core - x)
    last = jnp.int32(0)
    for (i, j), s in SLOT.items():
        last = jnp.where(jnp.logical_and(last_i == i, last_j == j), jnp.int32(s), last)
    for e in range(PIECES):
        p = e // 2 + (e % 2) * (PIECES // 2)
        r_copy(last, p).wait_recv()
        gout[:, p * piece : (p + 1) * piece] = (part[last, p] + zbuf[p]).astype(gout.dtype)
    give = pltpu.make_async_copy(gout, gin_ref, ls.at[3])
    give.start()

    for name in sent:
        arrivals[name[0]](*name[1:]).wait_send()

    def drain(s, carry):
        n, own, ahead, _ = place(s)

        @pl.when(jnp.logical_not(own))
        def _():
            d_copy(s, n).wait_send()

        @pl.when(jnp.logical_and(own, ahead != 0))
        def _():
            for p in range(PIECES):
                y_copy(s, n, 0, p).wait_send()

        return carry

    lax.fori_loop(0, 16, drain, 0)
    for p in range(PIECES):
        r_copy(last, p).wait_send()
    for r in range(4):
        out_copy(r).wait()
    give.wait()


def body(inputs, weight, grad_out):
    tokens, width = inputs.shape
    units = weight.shape[1]
    f32, bf16 = jnp.float32, jnp.bfloat16
    dma = pltpu.SemaphoreType.DMA
    blocks = (PIECES, tokens, width // PIECES)
    return pl.pallas_call(
        kernel,
        out_shape=(
            jax.ShapeDtypeStruct((tokens, width), bf16),
            jax.ShapeDtypeStruct((width, units), bf16),
        ),
        in_specs=[pl.BlockSpec(memory_space=pl.ANY)] * 3,
        out_specs=[pl.BlockSpec(memory_space=pl.ANY)] * 2,
        scratch_shapes=[
            pltpu.VMEM((16 * tokens, units), bf16),
            pltpu.VMEM((16, width, tokens), bf16),
            pltpu.VMEM((width, units), bf16),
            pltpu.VMEM((width, units), f32),
            pltpu.VMEM((16, *blocks), f32),
            pltpu.VMEM((8, *blocks), f32),
            pltpu.VMEM((8, 2, *blocks), f32),
            pltpu.VMEM(blocks, f32),
            pltpu.VMEM((width, units), bf16),
            pltpu.VMEM((tokens, width), bf16),
            pltpu.VMEM((tokens, width), bf16),
            dma((2, 4)), dma((2, 4)),
            dma((4, 2, 3)), dma((4, 2, 3)),
            dma((2, 2, 3)), dma((2, 2, 3)),
            dma, dma,
            dma((2, 5)), dma((2, 5)),
            dma((8,)), dma((8,)),
            dma((8, PIECES)), dma((8, 2, PIECES)),
            dma((PIECES,)), dma((PIECES,)),
            dma((4,)), dma((4,)),
        ],
        compiler_params=pltpu.CompilerParams(
            collective_id=0, has_side_effects=True, vmem_limit_bytes=58 * 2**20
        ),
        cost_estimate=pl.CostEstimate(
            flops=4 * 16 * tokens * width * units, bytes_accessed=2 * 2 * width * units, transcendentals=0
        ),
        name="feed_forward_backward",
    )(inputs, weight, grad_out)


def solution(mesh):
    return jax.shard_map(
        body,
        mesh=mesh,
        in_specs=(P("col", "row"), P("row", "col"), P("row", "col")),
        out_specs=(P("col", "row"), P("row", "col")),
        check_vma=False,
    )
```

time: 267 us -> 103 us (0.39)
  the two profiles are of different devices: /device:TPU:48 before, /device:TPU:21 now
where the time goes in v2:
time: 103 us
  Pallas kernels  96.9 us (94%)
  local copies, waits for them, and re-layouts  5.63 us (5%)
    pallas_call x1, Pallas kernels, body(): pl.pallas_call(kernel, out_shape=(jax.ShapeDtypeStruct((tokens, width), b...  96.9 us
    unnamed x2, local copies, waits for them, and re-layouts  5.63 us

profile of v2, /device:TPU:21, one launch (start us, length us, event | category | flops | bytes accessed | tf_op | source)
XLA Modules:
  0.0 103.2 jit_solution(6137451627568234878)
XLA Ops:
  0.6 96.9 %feed_forward_backward.1 = (bf16[128,1024]{1,0:T(8,128)(2,1)}, bf16[1024,1664]{1,0:T(8,128)(2,1)}) custom-call(bf16[128,1024]{1,0:T(8,128)(2,1)} %in_ref.1, bf16[1024,1664]{1,0:T(8,128)(2,1)} %w_ref.1, bf16[128,1664]{1,0:T(8,128)(2,1)} %go_ref.1), custom_call_target="tpu_custom_call" | custom-call | flops 13958643712 | bytes 6815744 | tf_op jit(solution)/shard_map/feed_forward_backward/pallas_call | solution.py:403
  97.5 1.7 %copy.7 = bf16[128,1024]{1,0:T(8,128)(2,1)} copy(bf16[128,1024]{1,0:T(8,128)(2,1)} %get-tuple-element.4) | data formatting | bytes 524288
  99.2 4.0 %copy.8 = bf16[1024,1664]{1,0:T(8,128)(2,1)} copy(bf16[1024,1664]{1,0:T(8,128)(2,1)} %get-tuple-element.5) | data formatting | bytes 6815744

commit v3 on v2

--- a/solution.py
+++ b/solution.py
@@ -7,6 +7,7 @@
 
 MESH = pl.DeviceIdType.MESH
 PIECES = 4
+SPANS = 8
 
 SLOTS = [
     (0, 0), (0, 1), (0, 3), (0, 2), (1, 0), (3, 0), (1, 1), (1, 3),
@@ -18,18 +19,18 @@
 RANK = [EVEN.index(s) if s in EVEN else ODD.index(s) for s in range(16)]
 
 ORDER = [
-    ("tf", 0, 0), ("tc", 0, 0), ("tf", 0, 1), ("fx", 0, 0), ("P", 0), ("fx", 0, 1), ("xa3",), ("xa1",), ("P", 1),
-    ("tl",), ("C", 1), ("P", 2), ("xb3",), ("zf", 1), ("P", 4), ("xb1",), ("fx", 3, 0), ("zf", 0), ("tr",),
-    ("tc", 0, 1), ("tg", 0, 1), ("C", 4), ("P", 5), ("P", 3), ("C", 5), ("P", 9), ("fx", 1, 1), ("tf", 1, 0),
-    ("tf", 1, 1), ("g", 1), ("C", 3), ("P", 8), ("g", 0), ("P", 6), ("C", 9), ("xa2",), ("P", 7), ("tc", 1, 0),
-    ("C", 6), ("C", 8), ("tg", 1, 1), ("C", 7), ("P", 10), ("C", 10), ("C", 0), ("tg", 0, 0), ("xb2",),
-    ("tg", 1, 0), ("F", 3), ("F", 9), ("F", 4), ("P", 11), ("P", 12), ("C", 11), ("fx", 2, 0), ("F", 5), ("F", 10),
-    ("tc", 1, 1), ("C", 12), ("fx", 2, 1), ("F", 8), ("P", 14), ("G", 0, 0), ("F", 1), ("G", 0, 1), ("P", 13),
-    ("N", 5), ("N", 3), ("C", 2), ("N", 9), ("C", 14), ("F", 11), ("F", 12), ("P", 15), ("N", 4), ("G", 0, 2),
-    ("C", 15), ("F", 2), ("G", 0, 3), ("G", 1, 0), ("F", 15), ("G", 1, 1), ("N", 8), ("N", 10), ("N", 12), ("F", 0),
-    ("C", 13), ("F", 7), ("F", 13), ("N", 11), ("N", 1), ("F", 14), ("G", 1, 2), ("G", 1, 3), ("F", 6), ("G", 2, 0),
-    ("N", 15), ("N", 7), ("N", 2), ("G", 2, 1), ("N", 6), ("G", 2, 2), ("N", 0), ("N", 14), ("G", 2, 3),
-    ("G", 3, 0), ("G", 3, 1), ("N", 13), ("G", 3, 2), ("G", 3, 3),
+    ("to",), ("xo",), ("tf", 0, 1), ("P", 0), ("fx", 0, 0), ("fx", 0, 1), ("zo",), ("xa1",), ("C", 0), ("xa3",),
+    ("tf", 0, 0), ("P", 3), ("C", 3), ("P", 2), ("tl",), ("P", 5), ("xb1",), ("xb3",), ("C", 5), ("zf", 1),
+    ("zf", 0), ("P", 4), ("C", 4), ("tr",), ("P", 6), ("F", 5), ("P", 7), ("tf", 1, 0), ("tg", 0, 0), ("fx", 3, 0),
+    ("C", 6), ("tf", 1, 1), ("P", 9), ("g", 0), ("xb2",), ("P", 10), ("C", 9), ("F", 0), ("xa2",), ("g", 1),
+    ("C", 10), ("C", 7), ("C", 2), ("P", 1), ("P", 8), ("C", 8), ("tc", 1, 0), ("fx", 1, 1), ("F", 6), ("F", 7),
+    ("F", 9), ("C", 1), ("tg", 0, 1), ("tc", 1, 1), ("F", 10), ("tc", 0, 1), ("P", 12), ("C", 12), ("F", 3),
+    ("fx", 2, 0), ("P", 13), ("F", 2), ("tc", 0, 0), ("tg", 1, 0), ("fx", 2, 1), ("C", 13), ("tg", 1, 1), ("P", 14),
+    ("P", 11), ("N", 6), ("F", 12), ("N", 10), ("N", 9), ("G", 0, 0), ("F", 8), ("G", 0, 1), ("F", 4), ("G", 0, 2),
+    ("N", 7), ("C", 11), ("F", 13), ("C", 14), ("P", 15), ("F", 1), ("N", 5), ("N", 8), ("N", 3), ("G", 0, 3),
+    ("N", 0), ("G", 1, 0), ("N", 2), ("N", 12), ("C", 15), ("G", 1, 1), ("G", 1, 2), ("N", 4), ("F", 15), ("N", 13),
+    ("F", 14), ("F", 11), ("G", 1, 3), ("G", 2, 0), ("N", 1), ("N", 14), ("G", 2, 1), ("N", 11), ("G", 2, 2),
+    ("G", 2, 3), ("N", 15), ("G", 3, 0), ("G", 3, 1), ("G", 3, 2), ("G", 3, 3),
 ]
 
 
@@ -122,8 +123,11 @@
         own = core == lax.rem(x + j, 2)
         return rank, own, lax.rem(zh + i - y + 8, 4), wrap(x + j) // 2
 
-    def d_copy(s, n):
-        return remote(part.at[s], dbuf.at[n], ds.at[n], dr.at[n], core_peer)
+    halves = PIECES // 2
+
+    def d_copy(s, n, h):
+        at = pl.ds(h * halves, halves)
+        return remote(part.at[s, at], dbuf.at[n, at], ds.at[n, h], dr.at[n, h], core_peer)
 
     def y_copy(s, n, d, p):
         return remote(part.at[s, p], ybuf.at[n, d, p], ys.at[n, p], yr.at[n, d, p], y_peer(1 - 2 * d))
@@ -145,24 +149,20 @@
     pl.semaphore_wait(barrier, 8)
 
     loads[0].wait()
-    for c in range(2):
-        for d in range(2):
-            z_copy(d, c).start()
-            x_copy(0, d, c).start()
+    for d in range(2):
+        z_copy(d, 0).start()
+        x_copy(0, d, 0).start()
     loads[1].wait()
     tin[kcol(y, 0, core)] = raw[...].T
-    for c in range(2):
-        for d in range(2):
-            t_copy(0, d, c).start()
+    for d in range(2):
+        t_copy(0, d, 0).start()
     t_core(0, 0).start()
     acc[...] = jnp.zeros_like(acc)
     loads[2].wait()
 
     arrivals = {"x": x_copy, "z": z_copy, "t": t_copy, "tl": t_zl, "tc": t_core}
     met = set()
-    sent = [("z", d, c) for d in range(2) for c in range(2)]
-    sent += [("x", 0, d, c) for d in range(2) for c in range(2)]
-    sent += [("t", 0, d, c) for d in range(2) for c in range(2)] + [("tc", 0, 0)]
+    sent = [name for d in range(2) for name in (("z", d, 0), ("x", 0, d, 0), ("t", 0, d, 0))] + [("tc", 0, 0)]
 
     def need(*names):
         for name in names:
@@ -191,25 +191,22 @@
 
         @pl.when(own)
         def _():
-            d_copy(s, n).wait_recv()
-
-            def add(p, carry):
-                part[s, p] += dbuf[n, p]
-                return carry
-
-            lax.fori_loop(0, PIECES, add, 0)
-
-            @pl.when(ahead == 2)
-            def _():
-                for p in range(PIECES // 2):
-                    y_copy(s, n, 0, p).start()
-                    y_copy(s, n, 1, PIECES // 2 + p).start()
-
-            @pl.when(jnp.logical_or(ahead == 1, ahead == 3))
-            def _():
-                d = ahead // 2
-                for p in range(PIECES // 2):
-                    y_copy(s, n, d, (1 - d) * (PIECES // 2) + p).start()
+            for h in range(2):
+                d_copy(s, n, h).wait_recv()
+
+                def add(e, carry):
+                    p = h * halves + e
+                    part[s, p] += dbuf[n, p]
+                    return carry
+
+                lax.fori_loop(0, halves, add, 0)
+
+                d = jnp.where(ahead == 2, h, 1 - h)
+
+                @pl.when(jnp.logical_or(ahead == 2, ahead == 3 - 2 * h))
+                def _():
+                    for e in range(halves):
+                        y_copy(s, n, d, h * halves + e).start()
 
     def sum_far(s):
         n, own, ahead, _ = place(s)
@@ -219,13 +216,13 @@
             d = ahead // 2
 
             def add(e, carry):
-                p = d * (PIECES // 2) + e
+                p = d * halves + e
                 y_copy(s, n, d, p).wait_recv()
                 part[s, p] += ybuf[n, d, p]
                 y_copy(s, n, d, p).start()
                 return carry
 
-            lax.fori_loop(0, PIECES // 2, add, 0)
+            lax.fori_loop(0, halves, add, 0)
 
     def sum_near(s):
         n, own, ahead, z_to = place(s)
@@ -233,7 +230,7 @@
         @pl.when(jnp.logical_and(own, ahead == 0))
         def _():
             def add(e, carry):
-                p = e // 2 + lax.rem(e, 2) * (PIECES // 2)
+                p = e // 2 + lax.rem(e, 2) * halves
                 for d in range(2):
                     y_copy(s, n, d, p).wait_recv()
                 part[s, p] += ybuf[n, 0, p] + ybuf[n, 1, p]
@@ -247,7 +244,13 @@
             lax.fori_loop(0, PIECES, add, 0)
 
     def light(kind, *at):
-        if kind == "fx":
+        if kind == "zo":
+            begin(("z", 0, 1), ("z", 1, 1))
+        elif kind == "xo":
+            begin(("x", 0, 0, 1), ("x", 0, 1, 1))
+        elif kind == "to":
+            begin(("t", 0, 0, 1), ("t", 0, 1, 1))
+        elif kind == "fx":
             need(("x", *at, 0))
             begin(("x", *at, 2))
         elif kind == "zf":
@@ -281,18 +284,18 @@
 
     def share(s):
         block = go[pl.ds(pl.multiple_of(s * tokens, tokens), tokens), :]
+        n, own, _, _ = place(s)
         for h in range(2):
             both = lax.dot_general(
                 block, w[pl.ds(h * (width // 2), width // 2), :], (((1,), (1,)), ((), ())),
                 preferred_element_type=jnp.float32,
             )
-            for e in range(PIECES // 2):
-                part[s, h * (PIECES // 2) + e] = both[:, e * piece : (e + 1) * piece]
-        n, own, _, _ = place(s)
-
-        @pl.when(jnp.logical_not(own))
-        def _():
-            d_copy(s, n).start()
+            for e in range(halves):
+                part[s, h * halves + e] = both[:, e * piece : (e + 1) * piece]
+
+            @pl.when(jnp.logical_not(own))
+            def _():
+                d_copy(s, n, h).start()
 
     tile = width // 4
 
@@ -363,7 +366,7 @@
     for (i, j), s in SLOT.items():
         last = jnp.where(jnp.logical_and(last_i == i, last_j == j), jnp.int32(s), last)
     for e in range(PIECES):
-        p = e // 2 + (e % 2) * (PIECES // 2)
+        p = e // 2 + (e % 2) * halves
         r_copy(last, p).wait_recv()
         gout[:, p * piece : (p + 1) * piece] = (part[last, p] + zbuf[p]).astype(gout.dtype)
     give = pltpu.make_async_copy(gout, gin_ref, ls.at[3])
@@ -377,7 +380,8 @@
 
         @pl.when(jnp.logical_not(own))
         def _():
-            d_copy(s, n).wait_send()
+            for h in range(2):
+                d_copy(s, n, h).wait_send()
 
         @pl.when(jnp.logical_and(own, ahead != 0))
         def _():
@@ -394,13 +398,28 @@
     give.wait()
 
 
+def hand_out(gin_held, gw_held, gin_ref, gw_ref, gin, gw, into, out):
+    rows = gw.shape[0] // SPANS
+    spans = [pl.ds(e * rows, rows) for e in range(SPANS)]
+    moves = [(gin_held, gin, gin_ref)] + [(gw_held.at[at], gw.at[at], gw_ref.at[at]) for at in spans]
+    reads = [pltpu.make_async_copy(a, b, into.at[e]) for e, (a, b, _) in enumerate(moves)]
+    writes = [pltpu.make_async_copy(b, c, out.at[e]) for e, (_, b, c) in enumerate(moves)]
+    for read in reads:
+        read.start()
+    for read, write in zip(reads, writes):
+        read.wait()
+        write.start()
+    for write in writes:
+        write.wait()
+
+
 def body(inputs, weight, grad_out):
     tokens, width = inputs.shape
     units = weight.shape[1]
     f32, bf16 = jnp.float32, jnp.bfloat16
     dma = pltpu.SemaphoreType.DMA
     blocks = (PIECES, tokens, width // PIECES)
-    return pl.pallas_call(
+    held = pl.pallas_call(
         kernel,
         out_shape=(
             jax.ShapeDtypeStruct((tokens, width), bf16),
@@ -425,7 +444,7 @@
             dma((2, 2, 3)), dma((2, 2, 3)),
             dma, dma,
             dma((2, 5)), dma((2, 5)),
-            dma((8,)), dma((8,)),
+            dma((8, 2)), dma((8, 2)),
             dma((8, PIECES)), dma((8, 2, PIECES)),
             dma((PIECES,)), dma((PIECES,)),
             dma((4,)), dma((4,)),
@@ -438,6 +457,22 @@
         ),
         name="feed_forward_backward",
     )(inputs, weight, grad_out)
+    return pl.pallas_call(
+        hand_out,
+        out_shape=(
+            jax.ShapeDtypeStruct((tokens, width), bf16),
+            jax.ShapeDtypeStruct((width, units), bf16),
+        ),
+        in_specs=[pl.BlockSpec(memory_space=pl.ANY)] * 2,
+        out_specs=[pl.BlockSpec(memory_space=pl.ANY)] * 2,
+        scratch_shapes=[
+            pltpu.VMEM((tokens, width), bf16),
+            pltpu.VMEM((width, units), bf16),
+            dma((SPANS + 1,)), dma((SPANS + 1,)),
+        ],
+        compiler_params=pltpu.CompilerParams(vmem_limit_bytes=58 * 2**20),
+        name="hand_out",
+    )(*held)
 
 
 def solution(mesh):

time: 103 us -> 95 us (0.922)
  the two profiles are of different devices: /device:TPU:21 before, /device:TPU:48 now
where the time goes in v3:
time: 95 us; the launch traced here: 93.8 us
  Pallas kernels  93.2 us (98%)
    pallas_call x1, Pallas kernels, body(): pl.pallas_call(kernel, out_shape=(jax.ShapeDtypeStruct((tokens, width), b...  89.9 us
    pallas_call x1, Pallas kernels, body(): pl.pallas_call(hand_out, out_shape=(jax.ShapeDtypeStruct((tokens, width),...  3.23 us

profile of v3, /device:TPU:48, one launch (start us, length us, event | category | flops | bytes accessed | tf_op | source)
XLA Modules:
  0.0 93.8 jit_solution(5987780244218625173)
XLA Ops:
  0.6 89.9 %feed_forward_backward.1 = (bf16[128,1024]{1,0:T(8,128)(2,1)}, bf16[1024,1664]{1,0:T(8,128)(2,1)}) custom-call(bf16[128,1024]{1,0:T(8,128)(2,1)} %in_ref.1, bf16[1024,1664]{1,0:T(8,128)(2,1)} %w_ref.1, bf16[128,1664]{1,0:T(8,128)(2,1)} %go_ref.1), custom_call_target="tpu_custom_call" | custom-call | flops 13958643712 | bytes 6815744 | tf_op jit(solution)/shard_map/feed_forward_backward/pallas_call | solution.py:422
  90.6 3.2 %hand_out.1 = (bf16[128,1024]{1,0:T(8,128)(2,1)}, bf16[1024,1664]{1,0:T(8,128)(2,1)}) custom-call(bf16[128,1024]{1,0:T(8,128)(2,1)} %get-tuple-element.4.gin_held, bf16[1024,1664]{1,0:T(8,128)(2,1)} %get-tuple-element.5.gw_held), custom_call_target="tpu_custom_call" | custom-call | tf_op jit(solution)/shard_map/hand_out/pallas_call | solution.py:460

commit v4 on v3

--- a/solution.py
+++ b/solution.py
@@ -7,7 +7,7 @@
 
 MESH = pl.DeviceIdType.MESH
 PIECES = 4
-SPANS = 8
+SPANS = 4
 
 SLOTS = [
     (0, 0), (0, 1), (0, 3), (0, 2), (1, 0), (3, 0), (1, 1), (1, 3),
@@ -21,7 +21,7 @@
 ORDER = [
     ("to",), ("xo",), ("tf", 0, 1), ("P", 0), ("fx", 0, 0), ("fx", 0, 1), ("zo",), ("xa1",), ("C", 0), ("xa3",),
     ("tf", 0, 0), ("P", 3), ("C", 3), ("P", 2), ("tl",), ("P", 5), ("xb1",), ("xb3",), ("C", 5), ("zf", 1),
-    ("zf", 0), ("P", 4), ("C", 4), ("tr",), ("P", 6), ("F", 5), ("P", 7), ("tf", 1, 0), ("tg", 0, 0), ("fx", 3, 0),
+    ("P", 4), ("zf", 0), ("C", 4), ("tr",), ("P", 6), ("F", 5), ("P", 7), ("tf", 1, 0), ("tg", 0, 0), ("fx", 3, 0),
     ("C", 6), ("tf", 1, 1), ("P", 9), ("g", 0), ("xb2",), ("P", 10), ("C", 9), ("F", 0), ("xa2",), ("g", 1),
     ("C", 10), ("C", 7), ("C", 2), ("P", 1), ("P", 8), ("C", 8), ("tc", 1, 0), ("fx", 1, 1), ("F", 6), ("F", 7),
     ("F", 9), ("C", 1), ("tg", 0, 1), ("tc", 1, 1), ("F", 10), ("tc", 0, 1), ("P", 12), ("C", 12), ("F", 3),
@@ -328,19 +328,23 @@
             waiting.append(t)
 
     def step(h, carry):
-        for at, tasks in enumerate(before):
-
-            @pl.when(h == at)
+        def prepare(at):
+            for t in before[at]:
+                light(*t)
+            if heavy[at][0] == "P":
+                need_block(heavy[at][1])
+            else:
+                need(*[("t", q, d, c) for q in range(2) for d in range(2) for c in range(3)], ("tl",))
+                need(*[("tc", q, e) for q in range(2) for e in range(5)])
+                for s in range(4 * heavy[at][1], 4 * heavy[at][1] + 4):
+                    need_block(s)
+
+        for group in range(0, len(heavy), 4):
+
+            @pl.when(jnp.logical_and(h >= group, h < group + 4))
             def _():
-                for t in tasks:
-                    light(*t)
-                if heavy[at][0] == "P":
-                    need_block(heavy[at][1])
-                else:
-                    need(*[("t", q, d, c) for q in range(2) for d in range(2) for c in range(3)], ("tl",))
-                    need(*[("tc", q, e) for q in range(2) for e in range(5)])
-                    for s in range(4 * heavy[at][1], 4 * heavy[at][1] + 4):
-                        need_block(s)
+                for at in range(group, min(group + 4, len(heavy))):
+                    pl.when(h == at)(lambda at=at: prepare(at))
 
         is_share = table(h, [t[0] == "P" for t in heavy]) == 1
 

time: 95 us -> 94.6 us (level)
  no operation moved by 1% of the time
where the time goes in v4:
time: 94.6 us; the launch traced here: 92.9 us
  Pallas kernels  92.3 us (98%)
    pallas_call x1, Pallas kernels, body(): pl.pallas_call(kernel, out_shape=(jax.ShapeDtypeStruct((tokens, width), b...  89.2 us
    pallas_call x1, Pallas kernels, body(): pl.pallas_call(hand_out, out_shape=(jax.ShapeDtypeStruct((tokens, width),...  3.09 us

profile of v4, /device:TPU:48, one launch (start us, length us, event | category | flops | bytes accessed | tf_op | source)
XLA Modules:
  0.0 92.9 jit_solution(17574989037903092428)
XLA Ops:
  0.6 89.2 %feed_forward_backward.1 = (bf16[128,1024]{1,0:T(8,128)(2,1)}, bf16[1024,1664]{1,0:T(8,128)(2,1)}) custom-call(bf16[128,1024]{1,0:T(8,128)(2,1)} %in_ref.1, bf16[1024,1664]{1,0:T(8,128)(2,1)} %w_ref.1, bf16[128,1664]{1,0:T(8,128)(2,1)} %go_ref.1), custom_call_target="tpu_custom_call" | custom-call | flops 13958643712 | bytes 6815744 | tf_op jit(solution)/shard_map/feed_forward_backward/pallas_call | solution.py:426
  89.8 3.1 %hand_out.1 = (bf16[128,1024]{1,0:T(8,128)(2,1)}, bf16[1024,1664]{1,0:T(8,128)(2,1)}) custom-call(bf16[128,1024]{1,0:T(8,128)(2,1)} %get-tuple-element.4.gin_held, bf16[1024,1664]{1,0:T(8,128)(2,1)} %get-tuple-element.5.gw_held), custom_call_target="tpu_custom_call" | custom-call | tf_op jit(solution)/shard_map/hand_out/pallas_call | solution.py:464
